TPU v7x, 32 devices: a whole 2x2x4 slice. The times are simulated.
32 devices in a mesh: row: 4 (over z), col: 8 (over y, x, core).
Axes of the slice: x: 2, y: 2, z: 4, core: 2. Of those that a mesh axis runs over, the one named last changes fastest.
Arguments:
- embeddings: bfloat16 [4096, 768], P(('row', 'col')), may hold values from -4 to 4
- neg_ids: int32 [4, 2048], P('row', 'col'), may hold values from 0 to 16383, as said below
- neg_counts: int32 [4], P('row'), may hold values from 256 to 2048, as said below
- index_rows: bfloat16 [16384, 768], P('row'), may hold values from -4 to 4
Outputs:
- row_loss: float32 [4096], P(('row', 'col'))
- grad: float32 [4096, 768], P(('row', 'col'))
Inputs may be any that keep to these rules, and one draw needn't show every extreme that they name: `neg_counts`: every entry lies within the range; some lists are full (2048) and some hold exactly 256 entries. Index shard of an id is id // 4096. Among the 256 slots of one device (neg_ids[b, c * 256 : (c + 1) * 256]) at most 128 ids belong to any one index shard, and in every such run exactly 128 belong to one of them.
All inputs are finite; a program needn't handle non-finite values.
Results may differ from a plain program's by a relative error of at most 0.00059.
Values may be sent and summed in bfloat16 or wider, within the bound.
A program may use at most 128 MiB of HBM per device.

v0:
```python
import jax
import jax.numpy as jnp
from jax import lax
from jax.sharding import PartitionSpec as P

D = 768


def per_device(embeddings, neg_ids, neg_counts, index_rows):
    scale = D ** (-0.5)
    n_col = lax.axis_size("col")
    shard_rows = embeddings.shape[0]
    width = embeddings.shape[1]
    row_id = lax.axis_index("row")
    col_id = lax.axis_index("col")
    queries = lax.all_gather(embeddings, "col", axis=0, tiled=True)
    keys = lax.all_gather(embeddings, "row", axis=0, tiled=True)
    query_count = queries.shape[0]
    key_count = keys.shape[0]
    requests = lax.all_gather(neg_ids, "row", axis=0, tiled=True)
    owned_count = index_rows.shape[0]
    slot_count = neg_ids.shape[1]
    local_ids = requests - row_id * owned_count
    owned = (local_ids >= 0) & (local_ids < owned_count)
    picked = jnp.take(index_rows, jnp.clip(local_ids, 0, owned_count - 1), axis=0)
    picked = jnp.where(owned[..., None], picked, jnp.zeros_like(picked))
    fetched = lax.psum_scatter(
        picked.astype(jnp.float32).astype(jnp.bfloat16), "row", scatter_dimension=0, tiled=True
    ).astype(jnp.float32)
    negatives = fetched[0].astype(jnp.bfloat16)
    row_glob = row_id * query_count + jnp.arange(query_count, dtype=jnp.int32)
    key_local = jnp.arange(key_count, dtype=jnp.int32)
    col_glob = (key_local // shard_rows * n_col + col_id) * shard_rows + key_local % shard_rows
    scores = jnp.dot(queries, keys.T, preferred_element_type=jnp.float32) * scale
    scores = jnp.where(row_glob[:, None] == col_glob[None, :], -jnp.inf, scores)
    slot_glob = col_id * slot_count + jnp.arange(slot_count, dtype=jnp.int32)
    hard = jnp.dot(queries, negatives.T, preferred_element_type=jnp.float32) * scale
    hard = jnp.where((slot_glob < neg_counts[0])[None, :], hard, -jnp.inf)
    local_top = jnp.maximum(jnp.max(scores, axis=1), jnp.max(hard, axis=1))
    top = lax.pmax(local_top, "col")
    partial_value = jnp.sum(jnp.exp(scores - top[:, None]), axis=1) + jnp.sum(
        jnp.exp(hard - top[:, None]), axis=1
    )
    total = lax.psum(partial_value, "col")
    lse = top + jnp.log(total)
    own_f = embeddings.astype(jnp.float32)
    partner = own_f.reshape(shard_rows // 2, 2, width)[:, ::-1].reshape(shard_rows, width)
    positive = jnp.sum(own_f * partner, axis=1) * scale
    own_lse = lax.dynamic_slice_in_dim(lse, col_id * shard_rows, shard_rows, 0)
    row_loss = own_lse - positive
    target = (jnp.bitwise_xor(row_glob, 1)[:, None] == col_glob[None, :]).astype(jnp.float32)
    probs_grad = (jnp.exp(scores - lse[:, None]) - target).astype(jnp.bfloat16)
    hard_probs = jnp.exp(hard - lse[:, None]).astype(jnp.bfloat16)
    term = jnp.dot(probs_grad, keys, preferred_element_type=jnp.float32)
    query_part = lax.psum_scatter(
        term + jnp.dot(hard_probs, negatives, preferred_element_type=jnp.float32),
        "col",
        scatter_dimension=0,
        tiled=True,
    )
    key_part = lax.psum_scatter(
        lax.dot_general(
            probs_grad, queries, (((0,), (0,)), ((), ())), preferred_element_type=jnp.float32
        ),
        "row",
        scatter_dimension=0,
        tiled=True,
    )
    grad = query_part + key_part
    return (row_loss, grad)


def solution(mesh):
    return jax.shard_map(
        per_device,
        mesh=mesh,
        in_specs=(P(("row", "col"), None), P("row", "col"), P("row"), P("row", None)),
        out_specs=(P(("row", "col")), P(("row", "col"), None)),
        check_vma=False,
    )
```

profile of v0, /device:TPU:0, one launch (start us, length us, event | category | flops | bytes accessed | tf_op | source)
XLA Modules:
  0.0 196.2 jit_solution(175145558935563326)
XLA Ops:
  8.0 0.0 all-gather.3.cloned.1.call-start
  8.0 0.7 all-gather.3.cloned.1.call-update
  8.7 0.0 reduce-scatter.4.cloned.1.call-start
  8.8 12.8 %all-gather = s32[4,1,256]{2,1,0:T(1,128)S(1)} all-gather(s32[1,1,256]{2,1,0:T(1,128)} %bitcast.31), channel_id=1, replica_groups=mesh['row'=4,'col'=8] {'row'}, dimensions={0}, use_global_device_ids=true | all-gather | bytes 5120 | tf_op jit(solution)/shard_map/all_gather | solution.py:20
  21.7 8.1 %gather_fusion = bf16[1024,768]{1,0:T(8,128)(2,1)S(1)} fusion(bf16[4096,768]{1,0:T(8,128)(2,1)} %param.7, s32[1024]{0:T(1024)S(1)} %broadcast_clamp_fusion), kind=kCustom, calls=%fused_computation | custom fusion | bytes 3149824 | tf_op jit(solution)/shard_map/jit(_take)/gather | solution.py:25
  29.8 0.0 copy-start
  29.8 1.4 select_select_fusion
  31.2 0.0 reduce-scatter.4.cloned.1.call-update
  31.2 0.0 reduce-scatter.8.cloned.1.call-start
  32.0 0.0 copy-done
  32.0 26.3 %all_gather.10 = bf16[512,768]{1,0:T(8,128)(2,1)S(1)} all-gather(bf16[128,768]{1,0:T(8,128)(2,1)S(1)} %copy-done), channel_id=1, replica_groups=mesh['row'=4,'col'=8] {'row'}, dimensions={0}, use_global_device_ids=true | all-gather | bytes 983040 | tf_op jit(solution)/shard_map/all_gather | solution.py:17
  58.3 0.0 copy-start.1
  58.3 0.0 all-gather.3.cloned.1.call-done
  58.3 2.7 %fusion.18 = (f32[1024]{0:T(1024)S(1)}, f32[1024,512]{0,1:T(8,128)S(1)}) fusion(bf16[1024,768]{1,0:T(8,128)(2,1)} %all-gather.3.cloned.1.call-done, bf16[512,768]{1,0:T(8,128)(2,1)S(1)} %all_gather.10, s32[512]{0:T(512)S(1)} %fusion.12, s32[1024]{0:T(1024)S(1)} %iota_add_fusion), kind=kOutput, calls=%fused_computation.43 | convolution fusion | flops 807402496 | bytes 4466688 | tf_op jit(solution)/shard_map/dot_general | solution.py:34
  61.0 0.0 copy-done.1
  61.0 12.1 %reduce-scatter.4.cloned.1.call-done = bf16[1,256,768]{2,1,0:T(8,128)(2,1)} async-done(((bf16[4,256,768]{2,1,0:T(8,128)(2,1)}), bf16[1,256,768]{2,1,0:T(8,128)(2,1)}) %reduce-scatter.4.cloned.1.call-update) | async-done | bytes 393232 | tf_op jit(solution)/shard_map/reduce_scatter | solution.py:27
  73.1 2.2 %fusion.19 = (f32[1024]{0:T(1024)S(1)}, f32[256,1024]{1,0:T(8,128)S(1)}) fusion(bf16[1024,768]{1,0:T(8,128)(2,1)} %all-gather.3.cloned.1.call-done, bf16[1,256,768]{2,1,0:T(8,128)(2,1)} %reduce-scatter.4.cloned.1.call-done, pred[256]{0:T(512)(128)(4,1)S(1)} %add_compare_fusion), kind=kOutput, calls=%fused_computation.44 | convolution fusion | flops 403438592 | bytes 3019008 | tf_op jit(solution)/shard_map/dot_general | solution.py:37
  75.3 14.0 %pmax.7 = f32[1024]{0:T(1024)S(1)} all-reduce(f32[1024]{0:T(1024)S(1)} %max.9), channel_id=1, replica_groups=mesh['row'=4,'col'=8] {'col'}, use_global_device_ids=true, to_apply=%region_3.4 | all-reduce | flops 1024 | bytes 8192 | tf_op jit(solution)/shard_map/pmax | solution.py:40
  89.2 0.2 exponential_reduce_fusion.1
  89.4 0.3 exponential_reduce_fusion
  89.7 11.8 %psum.7 = f32[1024]{0:T(1024)S(1)} all-reduce(f32[1024]{0:T(1024)S(1)} %add.93), channel_id=1, replica_groups=mesh['row'=4,'col'=8] {'col'}, use_global_device_ids=true, to_apply=%region_6.7 | all-reduce | flops 1024 | bytes 8192 | tf_op jit(solution)/shard_map/psum | solution.py:44
  101.5 3.8 %fusion.16 = f32[512,768]{1,0:T(8,128)} fusion(bf16[1024,768]{1,0:T(8,128)(2,1)} %all-gather.3.cloned.1.call-done, f32[1024,512]{0,1:T(8,128)S(1)} %get-tuple-element.3, s32[1024]{0:T(1024)S(1)} %broadcast_xor_fusion, f32[1024]{0:T(1024)S(1)} %log_add_fusion, s32[512]{0:T(512)S(1)} %fusion.12), kind=kOutput, calls=%fused_computation.41 | convolution fusion | flops 807927808 | bytes 5253120 | tf_op jit(solution)/shard_map/dot_general | solution.py:62
  105.3 0.0 reduce-scatter.8.cloned.1.call-update
  105.3 0.0 reduce-scatter.6.cloned.1.call-start
  105.4 0.0 copy-start.2
  105.4 2.3 %fusion.17 = f32[1024,768]{1,0:T(8,128)S(1)} fusion(bf16[512,768]{1,0:T(8,128)(2,1)} %copy-done.1, f32[1024,512]{0,1:T(8,128)S(1)} %get-tuple-element.3, s32[1024]{0:T(1024)S(1)} %broadcast_xor_fusion, f32[1024]{0:T(1024)S(1)} %log_add_fusion, s32[512]{0:T(512)S(1)} %fusion.12), kind=kOutput, calls=%fused_computation.42 | convolution fusion | flops 807927808 | bytes 6039552 | tf_op jit(solution)/shard_map/dot_general | solution.py:54
  107.7 0.0 copy-done.2
  107.7 2.3 %convolution_add_fusion = f32[1024,768]{1,0:T(8,128)} fusion(f32[1024,768]{1,0:T(8,128)S(1)} %fusion.17, f32[256,1024]{1,0:T(8,128)S(1)} %get-tuple-element.5, f32[1024]{0:T(1024)S(1)} %log_add_fusion, bf16[1,256,768]{2,1,0:T(8,128)(2,1)S(1)} %copy-done.2), kind=kOutput, calls=%fused_computation.4 | convolution fusion | flops 403963904 | bytes 7737344 | tf_op jit(solution)/shard_map/dot_general | solution.py:56
  110.0 0.0 reduce-scatter.6.cloned.1.call-update
  110.0 0.2 reshape.55
  110.2 1.1 rev.3
  111.4 0.3 reshape.56
  111.6 0.1 multiply_reduce_fusion
  111.8 0.6 multiply_subtract_fusion
  112.3 26.1 %reduce-scatter.8.cloned.1.call-done = f32[128,768]{1,0:T(8,128)} async-done(((f32[512,768]{1,0:T(8,128)}), f32[128,768]{1,0:T(8,128)}) %reduce-scatter.8.cloned.1.call-update) | async-done | bytes 393232 | tf_op jit(solution)/shard_map/reduce_scatter | solution.py:61
  138.4 48.2 %reduce-scatter.6.cloned.1.call-done = f32[128,768]{1,0:T(8,128)} async-done(((f32[1024,768]{1,0:T(8,128)}), f32[128,768]{1,0:T(8,128)}) %reduce-scatter.6.cloned.1.call-update) | async-done | bytes 393232 | tf_op jit(solution)/shard_map/reduce_scatter | solution.py:55
  186.7 1.9 add.97
  (14 shorter events, 0.1 us)
Async XLA Ops:
  8.0 50.3 %all-gather.3.cloned.1.call-start = ((), (), s32[]{:S(2)}) async-start(), calls=%async_computation.3 | async-start | bytes 1769472 | tf_op jit(solution)/shard_map/all_gather | solution.py:16
  8.7 64.4 %reduce-scatter.4.cloned.1.call-start = ((), (), s32[]{:S(2)}) async-start(), calls=%async_computation.4 | async-start | bytes 1966080 | tf_op jit(solution)/shard_map/reduce_scatter | solution.py:27
  29.8 2.2 %copy-start = (bf16[128,768]{1,0:T(8,128)(2,1)S(1)}, bf16[128,768]{1,0:T(8,128)(2,1)}, u32[]{:S(2)}) copy-start(bf16[128,768]{1,0:T(8,128)(2,1)} %param.4) | copy-start | bytes 589828
  31.2 107.2 %reduce-scatter.8.cloned.1.call-start = ((), (), s32[]{:S(2)}) async-start(), calls=%async_computation.6 | async-start | bytes 1966080 | tf_op jit(solution)/shard_map/reduce_scatter | solution.py:61
  58.3 2.7 %copy-start.1 = (bf16[512,768]{1,0:T(8,128)(2,1)}, bf16[512,768]{1,0:T(8,128)(2,1)S(1)}, u32[]{:S(2)}) copy-start(bf16[512,768]{1,0:T(8,128)(2,1)S(1)} %all_gather.10) | copy-start | bytes 2359300
  105.3 81.4 %reduce-scatter.6.cloned.1.call-start = ((), (), s32[]{:S(2)}) async-start(), calls=%async_computation.5 | async-start | bytes 3538944 | tf_op jit(solution)/shard_map/reduce_scatter | solution.py:55
  105.4 2.3 %copy-start.2 = (bf16[1,256,768]{2,1,0:T(8,128)(2,1)S(1)}, bf16[1,256,768]{2,1,0:T(8,128)(2,1)}, u32[]{:S(2)}) copy-start(bf16[1,256,768]{2,1,0:T(8,128)(2,1)} %reduce-scatter.4.cloned.1.call-done) | copy-start | bytes 1179652
Sparse Core Ops, SparseCore 0:
  10.7 28.4 all-gather.2
Sparse Core Ops, SparseCore 1:
  31.3 41.7 reduce-scatter.3
  105.4 33.0 reduce-scatter.7
  141.7 44.9 reduce-scatter.5
where the time goes:
time: 197 us; the launch traced here: 196 us
  waiting for transfers between devices  87.1 us (44%)
  blocking collectives  64.9 us (33%)
  between operations  16.5 us (8%)
  matrix products  13.3 us (7%)
  local copies, waits for them, and re-layouts  9.65 us (5%)
  other arithmetic  4.59 us (2%)
    reduce_scatter x1, waiting for transfers between devices, per_device(): lax.psum_scatter(term + jnp.dot(hard_probs, negatives, preferred_element_...  48.2 us
    all_gather x1, blocking collectives, per_device(): keys = lax.all_gather(embeddings, 'row', axis=0, tiled=True)  26.3 us
    reduce_scatter x1, waiting for transfers between devices, per_device(): lax.psum_scatter(lax.dot_general(probs_grad, queries, (((0,), (0,)), ((),...  26.1 us
    pmax x1, blocking collectives, per_device(): top = lax.pmax(local_top, 'col')  14 us
    all_gather x1, blocking collectives, per_device(): requests = lax.all_gather(neg_ids, 'row', axis=0, tiled=True)  12.8 us
    reduce_scatter x1, waiting for transfers between devices, per_device(): lax.psum_scatter(picked.astype(jnp.float32).astype(jnp.bfloat16), 'row',...  12.1 us
    psum x1, blocking collectives, per_device(): total = lax.psum(partial_value, 'col')  11.8 us
    gather x1, local copies, waits for them, and re-layouts, per_device(): jnp.take(index_rows, jnp.clip(local_ids, 0, owned_count - 1), axis=0)  8.07 us
  transfers between devices with their start and end apart: 4, of which 3 were waited for; matrix products, arithmetic and copies ran while one was open for 10% of the time, Pallas kernels for 0%

commit v1 on v0

--- a/solution.py
+++ b/solution.py
@@ -14,7 +14,14 @@
     row_id = lax.axis_index("row")
     col_id = lax.axis_index("col")
     queries = lax.all_gather(embeddings, "col", axis=0, tiled=True)
-    keys = lax.all_gather(embeddings, "row", axis=0, tiled=True)
+    size = lax.axis_size("row")
+    right = [(i, (i + 1) % size) for i in range(size)]
+    parts = [embeddings]
+    for far in range(1, size):
+        parts = [lax.ppermute(parts[0], "row", right), *parts]
+    whole = jnp.concatenate(parts, axis=0)
+    shift = (lax.axis_index("row") + 1) * parts[-1].shape[0]
+    keys = jnp.roll(whole, shift, axis=0)
     query_count = queries.shape[0]
     key_count = keys.shape[0]
     requests = lax.all_gather(neg_ids, "row", axis=0, tiled=True)

time: 197 us -> 197 us (level)
  blocking collectives: 64.9 us -> 38.5 us
  waiting for transfers between devices: 87.1 us -> 107 us
  local copies, waits for them, and re-layouts: 9.65 us -> 16 us
    ppermute x0 -> x3, waiting for transfers between devices: none -> 31.4 us  [per_device(): parts = [lax.ppermute(parts[0], 'row', right), *parts]]
    all_gather x1 -> x0, blocking collectives: 26.3 us -> none  [per_device(): keys = lax.all_gather(embeddings, 'row', axis=0, tiled=True)]
    reduce_scatter x1, waiting for transfers between devices: 12.1 us -> 1.74 us  [per_device(): lax.psum_scatter(picked.astype(jnp.float32).astype(jnp.bfloat16), 'row',...]
    unnamed x8 -> x11, local copies, waits for them, and re-layouts: 0.02 us -> 5.72 us
  transfers between devices with their start and end apart: 4 -> 7, of which waited for: 3 -> 6; matrix products, arithmetic and copies ran while one was open for 10% -> 13% of each run, Pallas kernels for 0% -> 0%
where the time goes in v1:
time: 197 us
  waiting for transfers between devices  107 us (54%)
  blocking collectives  38.5 us (20%)
  between operations  16.5 us (8%)
  local copies, waits for them, and re-layouts  16 us (8%)
  matrix products  14.2 us (7%)
  other arithmetic  4.6 us (2%)
    reduce_scatter x1, waiting for transfers between devices, per_device(): lax.psum_scatter(term + jnp.dot(hard_probs, negatives, preferred_element_...  48.3 us
    ppermute x3, waiting for transfers between devices, per_device(): parts = [lax.ppermute(parts[0], 'row', right), *parts]  31.4 us
    reduce_scatter x1, waiting for transfers between devices, per_device(): lax.psum_scatter(lax.dot_general(probs_grad, queries, (((0,), (0,)), ((),...  24.7 us
    pmax x1, blocking collectives, per_device(): top = lax.pmax(local_top, 'col')  13.9 us
    all_gather x1, blocking collectives, per_device(): requests = lax.all_gather(neg_ids, 'row', axis=0, tiled=True)  12.8 us
    psum x1, blocking collectives, per_device(): total = lax.psum(partial_value, 'col')  11.8 us
    gather x1, local copies, waits for them, and re-layouts, per_device(): jnp.take(index_rows, jnp.clip(local_ids, 0, owned_count - 1), axis=0)  8.07 us
    unnamed x11, local copies, waits for them, and re-layouts  5.72 us
  transfers between devices with their start and end apart: 7, of which 6 were waited for; matrix products, arithmetic and copies ran while one was open for 13% of the time, Pallas kernels for 0%

profile of v1, /device:TPU:0, one launch (start us, length us, event | category | flops | bytes accessed | tf_op | source)
XLA Modules:
  0.0 196.9 jit_solution(15286123292843201838)
XLA Ops:
  8.0 0.0 all-gather.3.cloned.1.call-start
  8.0 0.7 all-gather.3.cloned.1.call-update
  8.7 0.0 reduce-scatter.4.cloned.1.call-start
  8.8 12.8 %all-gather = s32[4,1,256]{2,1,0:T(1,128)S(1)} all-gather(s32[1,1,256]{2,1,0:T(1,128)} %bitcast.31), channel_id=1, replica_groups=mesh['row'=4,'col'=8] {'row'}, dimensions={0}, use_global_device_ids=true | all-gather | bytes 5120 | tf_op jit(solution)/shard_map/all_gather | solution.py:27
  21.7 8.1 %gather_fusion = bf16[1024,768]{1,0:T(8,128)(2,1)S(1)} fusion(bf16[4096,768]{1,0:T(8,128)(2,1)} %param.7, s32[1024]{0:T(1024)S(1)} %broadcast_clamp_fusion), kind=kCustom, calls=%fused_computation | custom fusion | bytes 3149824 | tf_op jit(solution)/shard_map/jit(_take)/gather | solution.py:32
  29.8 1.4 select_select_fusion
  31.2 0.0 copy-start
  31.2 0.0 reduce-scatter.4.cloned.1.call-update
  31.2 0.0 reduce-scatter.8.cloned.1.call-start
  31.3 0.8 copy-done
  32.1 0.0 collective-permute-start
  32.8 7.1 %collective-permute-done = bf16[128,768]{1,0:T(8,128)(2,1)S(1)} collective-permute-done((bf16[128,768]{1,0:T(8,128)(2,1)S(1)}, bf16[128,768]{1,0:T(8,128)(2,1)S(1)}, u32[]{:S(2)}, u32[]{:S(2)}) %collective-permute-start) | collective-permute-done | bytes 196640 | tf_op jit(solution)/shard_map/ppermute | solution.py:21
  39.9 0.0 collective-permute-start.1
  40.0 12.2 %collective-permute-done.1 = bf16[128,768]{1,0:T(8,128)(2,1)S(1)} collective-permute-done((bf16[128,768]{1,0:T(8,128)(2,1)S(1)}, bf16[128,768]{1,0:T(8,128)(2,1)S(1)}, u32[]{:S(2)}, u32[]{:S(2)}) %collective-permute-start.1) | collective-permute-done | bytes 196640 | tf_op jit(solution)/shard_map/ppermute | solution.py:21
  52.1 0.0 collective-permute-start.2
  52.2 12.1 %collective-permute-done.2 = bf16[128,768]{1,0:T(8,128)(2,1)S(1)} collective-permute-done((bf16[128,768]{1,0:T(8,128)(2,1)S(1)}, bf16[128,768]{1,0:T(8,128)(2,1)S(1)}, u32[]{:S(2)}, u32[]{:S(2)}) %collective-permute-start.2) | collective-permute-done | bytes 196640 | tf_op jit(solution)/shard_map/ppermute | solution.py:21
  64.3 0.7 constant_dynamic-update-slice_fusion.7
  64.9 0.7 constant_dynamic-update-slice_fusion.6
  65.6 0.7 constant_dynamic-update-slice_fusion.5
  66.3 0.7 constant_dynamic-update-slice_fusion.4
  67.0 0.7 constant_dynamic-update-slice_fusion.3
  67.7 0.7 constant_dynamic-update-slice_fusion.2
  68.4 0.7 constant_dynamic-update-slice_fusion.1
  69.1 0.7 constant_dynamic-update-slice_fusion
  69.8 0.0 all-gather.3.cloned.1.call-done
  69.8 2.7 %fusion.22 = (f32[1024]{0:T(1024)S(1)}, f32[1024,512]{0,1:T(8,128)S(1)}) fusion(bf16[1024,768]{1,0:T(8,128)(2,1)} %all-gather.3.cloned.1.call-done, bf16[1024,768]{1,0:T(8,128)(2,1)} %constant_dynamic-update-slice_fusion, s32[]{:T(128)S(6)} %select_n.60, s32[512]{0:T(512)S(1)} %fusion.15, s32[1024]{0:T(1024)S(1)} %iota_add_fusion), kind=kOutput, calls=%fused_computation.55 | convolution fusion | flops 807402496 | bytes 4466692 | tf_op jit(solution)/shard_map/dot_general | solution.py:41
  72.5 1.7 reduce-scatter.4.cloned.1.call-done
  74.2 2.2 %fusion.23 = (f32[1024]{0:T(1024)S(1)}, f32[256,1024]{1,0:T(8,128)S(1)}) fusion(bf16[1024,768]{1,0:T(8,128)(2,1)} %all-gather.3.cloned.1.call-done, bf16[1,256,768]{2,1,0:T(8,128)(2,1)} %reduce-scatter.4.cloned.1.call-done, pred[256]{0:T(512)(128)(4,1)S(1)} %add_compare_fusion), kind=kOutput, calls=%fused_computation.56 | convolution fusion | flops 403438592 | bytes 3019008 | tf_op jit(solution)/shard_map/dot_general | solution.py:44
  76.4 13.9 %pmax.7 = f32[1024]{0:T(1024)S(1)} all-reduce(f32[1024]{0:T(1024)S(1)} %max.9), channel_id=1, replica_groups=mesh['row'=4,'col'=8] {'col'}, use_global_device_ids=true, to_apply=%region_3.4 | all-reduce | flops 1024 | bytes 8192 | tf_op jit(solution)/shard_map/pmax | solution.py:47
  90.3 0.2 exponential_reduce_fusion.1
  90.5 0.3 exponential_reduce_fusion
  90.8 11.8 %psum.7 = f32[1024]{0:T(1024)S(1)} all-reduce(f32[1024]{0:T(1024)S(1)} %add.109), channel_id=1, replica_groups=mesh['row'=4,'col'=8] {'col'}, use_global_device_ids=true, to_apply=%region_6.7 | all-reduce | flops 1024 | bytes 8192 | tf_op jit(solution)/shard_map/psum | solution.py:51
  102.6 3.8 %fusion.21 = f32[512,768]{1,0:T(8,128)} fusion(bf16[1024,768]{1,0:T(8,128)(2,1)} %all-gather.3.cloned.1.call-done, f32[1024,512]{0,1:T(8,128)S(1)} %get-tuple-element.3, s32[1024]{0:T(1024)S(1)} %broadcast_xor_fusion, f32[1024]{0:T(1024)S(1)} %log_add_fusion, s32[512]{0:T(512)S(1)} %fusion.15), kind=kOutput, calls=%fused_computation.54 | convolution fusion | flops 807927808 | bytes 5253120 | tf_op jit(solution)/shard_map/dot_general | solution.py:69
  106.4 0.0 reduce-scatter.8.cloned.1.call-update
  106.4 0.0 reduce-scatter.6.cloned.1.call-start
  106.5 1.6 fusion.3
  108.1 4.0 %convolution_add_fusion = f32[1024,768]{1,0:T(8,128)} fusion(f32[1024,768]{1,0:T(8,128)S(1)} %fusion.3, bf16[1024,768]{1,0:T(8,128)(2,1)} %constant_dynamic-update-slice_fusion, s32[]{:T(128)S(6)} %select_n.60, f32[1024,512]{0,1:T(8,128)S(1)} %get-tuple-element.3, s32[1024]{0:T(1024)S(1)} %broadcast_xor_fusion, f32[1024]{0:T(1024)S(1)} %log_add_fusion, ...), kind=kOutput, calls=%fused_computation.4 | convolution fusion | flops 808714240 | bytes 9185284 | tf_op jit(solution)/shard_map/dot_general | solution.py:61
  112.1 0.0 reduce-scatter.6.cloned.1.call-update
  112.1 0.2 reshape.55
  112.3 1.1 rev.3
  113.4 0.3 reshape.56
  113.7 0.1 multiply_reduce_fusion
  113.8 0.6 multiply_subtract_fusion
  114.4 24.7 %reduce-scatter.8.cloned.1.call-done = f32[128,768]{1,0:T(8,128)} async-done(((f32[512,768]{1,0:T(8,128)}), f32[128,768]{1,0:T(8,128)}) %reduce-scatter.8.cloned.1.call-update) | async-done | bytes 393232 | tf_op jit(solution)/shard_map/reduce_scatter | solution.py:68
  139.1 48.3 %reduce-scatter.6.cloned.1.call-done = f32[128,768]{1,0:T(8,128)} async-done(((f32[1024,768]{1,0:T(8,128)}), f32[128,768]{1,0:T(8,128)}) %reduce-scatter.6.cloned.1.call-update) | async-done | bytes 393232 | tf_op jit(solution)/shard_map/reduce_scatter | solution.py:62
  187.4 1.9 add.113
  (14 shorter events, 0.1 us)
Async XLA Ops:
  8.0 61.8 %all-gather.3.cloned.1.call-start = ((), (), s32[]{:S(2)}) async-start(), calls=%async_computation.3 | async-start | bytes 1769472 | tf_op jit(solution)/shard_map/all_gather | solution.py:16
  8.7 65.5 %reduce-scatter.4.cloned.1.call-start = ((), (), s32[]{:S(2)}) async-start(), calls=%async_computation.4 | async-start | bytes 1966080 | tf_op jit(solution)/shard_map/reduce_scatter | solution.py:34
  31.2 0.9 copy-start
  31.2 107.9 %reduce-scatter.8.cloned.1.call-start = ((), (), s32[]{:S(2)}) async-start(), calls=%async_computation.6 | async-start | bytes 1966080 | tf_op jit(solution)/shard_map/reduce_scatter | solution.py:68
  32.1 7.8 %collective-permute-start = (bf16[128,768]{1,0:T(8,128)(2,1)S(1)}, bf16[128,768]{1,0:T(8,128)(2,1)S(1)}, u32[]{:S(2)}, u32[]{:S(2)}) collective-permute-start(bf16[128,768]{1,0:T(8,128)(2,1)S(1)} %copy-done), channel_id=1, source_target_pairs={{0,8},{8,16},{16,24},{24,0},{1,9},{9,17},{17,25},{25,1},{2,10},{10... | collective-permute-start | bytes 589832 | tf_op jit(solution)/shard_map/ppermute | solution.py:21
  39.9 12.2 %collective-permute-start.1 = (bf16[128,768]{1,0:T(8,128)(2,1)S(1)}, bf16[128,768]{1,0:T(8,128)(2,1)S(1)}, u32[]{:S(2)}, u32[]{:S(2)}) collective-permute-start(bf16[128,768]{1,0:T(8,128)(2,1)S(1)} %collective-permute-done), channel_id=1, source_target_pairs={{0,8},{8,16},{16,24},{24,0},{1,9},{9,17},{17,25},{25,1},{2,10},{10... | collective-permute-start | bytes 589832 | tf_op jit(solution)/shard_map/ppermute | solution.py:21
  52.1 12.1 %collective-permute-start.2 = (bf16[128,768]{1,0:T(8,128)(2,1)S(1)}, bf16[128,768]{1,0:T(8,128)(2,1)S(1)}, u32[]{:S(2)}, u32[]{:S(2)}) collective-permute-start(bf16[128,768]{1,0:T(8,128)(2,1)S(1)} %collective-permute-done.1), channel_id=1, source_target_pairs={{0,8},{8,16},{16,24},{24,0},{1,9},{9,17},{17,25},{25,1},{2,10},{10... | collective-permute-start | bytes 589832 | tf_op jit(solution)/shard_map/ppermute | solution.py:21
  106.4 81.0 %reduce-scatter.6.cloned.1.call-start = ((), (), s32[]{:S(2)}) async-start(), calls=%async_computation.5 | async-start | bytes 3538944 | tf_op jit(solution)/shard_map/reduce_scatter | solution.py:62
Sparse Core Ops, SparseCore 0:
  10.7 28.3 all-gather.2
Sparse Core Ops, SparseCore 1:
  31.3 42.9 reduce-scatter.3
  106.5 32.5 reduce-scatter.7
  142.3 45.0 reduce-scatter.5
